TPU v7x, 128 devices: a whole 4x4x4 slice. The times are simulated.
128 devices in a mesh: seq: 64 (over z, y, x), head: 2 (over core), dp: 1.
Axes of the slice: x: 4, y: 4, z: 4, core: 2. Of those that a mesh axis runs over, the one named last changes fastest.
Arguments:
- tokens: bfloat16 [16384, 3072], P(('dp', 'seq'), 'head'), may hold values from -22 to 22
- clip_id: int32 [16384], P(('dp', 'seq')), may hold values from 0 to 2, never falling along the last dimension, each value on 1 to 10240 neighbouring positions
- w_qkv: bfloat16 [3, 3072, 1536], P(None, None, 'head'), may hold values from -0.109375 to 0.109375
- w_out: bfloat16 [1536, 3072], P('head'), may hold values from -0.15625 to 0.15625
Outputs:
- output_rows: bfloat16 [16384, 3072], P(('dp', 'seq'), 'head')
Inputs may be any that keep to these rules, and one draw needn't show every extreme that they name: `clip_id`: clip numbers never fall along the rows; each clip holds 1 to 10240 rows and one holds exactly 10240.
All inputs are finite; a program needn't handle non-finite values.
Results may differ from a plain program's by a relative error of at most 0.015.
Values may be sent and summed in bfloat16 or wider, within the bound.
No kernel may reach another device: no remote copies, remote signals or barrier semaphores. Data moves between devices by JAX's collectives and lax.ppermute only.
A program may use at most 192 MiB of HBM per device.

v0:
```python
import math

import jax
import jax.numpy as jnp
from jax import lax
from jax.sharding import PartitionSpec as P

HEAD_DIM = 128


def body(tokens, clip_id, w_qkv, w_out):
    row_count = tokens.shape[0]
    head_cols = w_qkv.shape[2]
    local_heads = head_cols // HEAD_DIM
    score_scale = 1.0 / math.sqrt(HEAD_DIM)
    stacked = jnp.einsum(
        "td,sdc->stc",
        lax.all_gather(tokens, "head", axis=1, tiled=True),
        w_qkv,
        preferred_element_type=jnp.float32,
    )
    stacked = stacked.astype(jnp.bfloat16)
    queries = stacked[0].reshape(row_count, local_heads, HEAD_DIM)
    keys_flat = stacked[1]
    values_flat = stacked[2]

    def attend_tile(state_now, tile_set):
        key_tile, value_tile, clip_tile = tile_set
        key_rows = key_tile.shape[0]
        key_heads = key_tile.reshape(key_rows, local_heads, HEAD_DIM)
        value_heads = value_tile.reshape(key_rows, local_heads, HEAD_DIM)
        running, totals, accumulated = state_now
        scores = (
            jnp.einsum("qhd,khd->qhk", queries, key_heads, preferred_element_type=jnp.float32)
            * score_scale
        )
        allowed = (clip_id[:, None] == clip_tile[None, :])[:, None, :]
        scores = jnp.where(allowed, scores, -1e30)
        highest = jnp.maximum(running, jnp.max(scores, axis=-1))
        weights = jnp.where(allowed, jnp.exp(scores - highest[..., None]), 0.0)
        factor = jnp.exp(running - highest)
        totals = totals * factor + jnp.sum(weights, axis=-1)
        accumulated = accumulated * factor[..., None] + jnp.einsum(
            "qhk,khd->qhd",
            weights.astype(jnp.bfloat16),
            value_heads,
            preferred_element_type=jnp.float32,
        )
        return (highest, totals, accumulated)

    initial = (
        jnp.full((row_count, local_heads), -1e30, jnp.float32),
        jnp.zeros((row_count, local_heads), jnp.float32),
        jnp.zeros((row_count, local_heads, HEAD_DIM), jnp.float32),
    )
    key_piece = lax.all_gather(keys_flat, "seq", axis=0, tiled=True)
    value_piece = lax.all_gather(values_flat, "seq", axis=0, tiled=True)
    clip_piece = lax.all_gather(clip_id, "seq", axis=0, tiled=True)
    piece_rows = key_piece.shape[0]
    tile_rows = math.gcd(piece_rows, 512)
    tile_count = piece_rows // tile_rows
    tiles = (
        key_piece.reshape(tile_count, tile_rows, head_cols),
        value_piece.reshape(tile_count, tile_rows, head_cols),
        clip_piece.reshape(tile_count, tile_rows),
    )

    def tile_step(running_state, tile_set):
        return (attend_tile(running_state, tile_set), None)

    result, unused = lax.scan(tile_step, initial, tiles)
    running, totals, accumulated = result
    attended = (accumulated / totals[..., None]).astype(jnp.bfloat16).reshape(row_count, head_cols)
    partial_sums = jnp.dot(attended, w_out, preferred_element_type=jnp.float32)
    combined = lax.psum_scatter(
        partial_sums.astype(jnp.bfloat16), "head", scatter_dimension=1, tiled=True
    )
    return combined


def solution(mesh):
    in_specs = (P(("dp", "seq"), "head"), P(("dp", "seq")), P(None, None, "head"), P("head", None))
    out_specs = P(("dp", "seq"), "head")
    return jax.shard_map(body, mesh=mesh, in_specs=in_specs, out_specs=out_specs, check_vma=False)
```

profile of v0, /device:TPU:1, one launch (start us, length us, event | category | flops | bytes accessed | tf_op | source)
XLA Modules:
  0.0 707.9 jit_solution(12627458745564697430)
XLA Ops:
  7.3 17.9 %all-gather.7.cloned.1.call-done = bf16[256,3072]{1,0:T(8,128)(2,1)} async-done(((bf16[256,1536]{1,0:T(8,128)(2,1)}), bf16[256,3072]{1,0:T(8,128)(2,1)}) %all-gather.7.cloned.1.call-update) | async-done | bytes 1572880 | tf_op jit(solution)/shard_map/all_gather | solution.py:18
  25.2 9.3 %fusion.21 = bf16[3,256,768]{1,2,0:T(8,128)(2,1)S(1)} fusion(bf16[3,3072,768]{2,1,0:T(8,128)(2,1)} %param.8, bf16[256,3072]{1,0:T(8,128)(2,1)} %all-gather.7.cloned.1.call-done), kind=kOutput, calls=%fused_computation.25 | convolution fusion | flops 3624468480 | bytes 16908288 | tf_op jit(solution)/shard_map/td,sdc->stc/dot_general | solution.py:16
  36.3 148.9 %all-gather.2 = s32[64,1,256]{2,1,0:T(1,128)S(1)} all-gather(s32[1,1,256]{2,1,0:T(1,128)S(1)} %bitcast.79), channel_id=1, replica_groups=mesh['seq'=64,'head'=2,'dp'=1] {'seq'}, dimensions={0}, use_global_device_ids=true | all-gather | bytes 66560 | tf_op jit(solution)/shard_map/all_gather | solution.py:58
  186.4 33.7 %all-gather.9.cloned.1.call-done = bf16[1,16384,768]{1,2,0:T(8,128)(2,1)} async-done(((bf16[1,256,768]{1,2,0:T(8,128)(2,1)}), bf16[1,16384,768]{1,2,0:T(8,128)(2,1)}) %all-gather.9.cloned.1.call-update) | async-done | bytes 25165840 | tf_op jit(solution)/shard_map/all_gather | solution.py:56
  220.1 17.7 %copy.25 = bf16[96,8,32,512]{3,2,1,0:T(8,128)(2,1)S(1)} copy(bf16[96,8,32,512]{3,1,2,0:T(8,128)(2,1)} %bitcast.73) | data formatting | bytes 50331648
  237.8 44.3 %copy.19 = bf16[32,512,768]{1,2,0:T(8,128)(2,1)} copy(bf16[32,512,768]{1,0,2:T(8,128)(2,1)S(1)} %bitcast.70) | data formatting | bytes 50331648
  282.1 125.4 %all-gather.11.cloned.1.call-done = bf16[1,16384,768]{1,2,0:T(8,128)(2,1)} async-done(((bf16[1,256,768]{1,2,0:T(8,128)(2,1)}), bf16[1,16384,768]{1,2,0:T(8,128)(2,1)}) %all-gather.11.cloned.1.call-update) | async-done | bytes 25165840 | tf_op jit(solution)/shard_map/all_gather | solution.py:57
  407.5 17.6 %copy.26 = bf16[96,8,32,512]{3,2,1,0:T(8,128)(2,1)S(1)} copy(bf16[96,8,32,512]{3,1,2,0:T(8,128)(2,1)} %bitcast.74) | data formatting | bytes 50331648
  425.1 44.4 %copy.21 = bf16[32,512,768]{1,2,0:T(8,128)(2,1)} copy(bf16[32,512,768]{1,0,2:T(8,128)(2,1)S(1)} %bitcast.71) | data formatting | bytes 50331648
  469.5 211.8 %while.15 = (s32[]{:T(128)}, f32[256,6]{0,1:T(8,128)S(1)}, f32[256,6]{0,1:T(8,128)S(1)}, f32[256,6,128]{0,2,1:T(8,128)}, s32[256]{0:T(256)S(1)}, /*index=5*/s32[...) while((s32[]{:T(128)}, f32[256,6]{0,1:T(8,128)S(1)}, ...), condition=%wide.region_3.4_spmd.clone, body=%wide.region_0.3_spmd.clone.sunk | while | flops 413605376 | bytes 27761904 | solution.py:71
  469.6 2.3 constant_dynamic-slice_fusion.6
  476.2 2.3 constant_dynamic-slice_fusion.6
  489.5 2.3 constant_dynamic-slice_fusion.6
  509.3 2.3 constant_dynamic-slice_fusion.6
  522.6 2.3 constant_dynamic-slice_fusion.6
  542.4 2.3 constant_dynamic-slice_fusion.6
  562.3 2.3 constant_dynamic-slice_fusion.6
  575.5 2.3 constant_dynamic-slice_fusion.6
  582.2 2.3 constant_dynamic-slice_fusion.6
  595.4 2.3 constant_dynamic-slice_fusion.6
  615.2 2.3 constant_dynamic-slice_fusion.6
  635.1 2.3 constant_dynamic-slice_fusion.6
  682.5 4.9 convolution_convert_fusion
  687.4 14.0 %reduce-scatter.2.cloned.1.call-done = bf16[256,1536]{1,0:T(8,128)(2,1)} async-done(((bf16[256,3072]{1,0:T(8,128)(2,1)}), bf16[256,1536]{1,0:T(8,128)(2,1)}) %reduce-scatter.2.cloned.1.call-update) | async-done | bytes 786448 | tf_op jit(solution)/shard_map/reduce_scatter | solution.py:75
  (550 shorter events, 186.0 us)
Async XLA Ops:
  6.5 18.7 %all-gather.7.cloned.1.call-start = ((), (), s32[]{:S(2)}) async-start(), calls=%async_computation.1 | async-start | bytes 2359296 | tf_op jit(solution)/shard_map/all_gather | solution.py:18
  7.3 212.8 %all-gather.9.cloned.1.call-start = ((), (), s32[]{:S(2)}) async-start(), calls=%async_computation.3 | async-start | bytes 25559040 | tf_op jit(solution)/shard_map/all_gather | solution.py:56
  35.5 372.0 %all-gather.11.cloned.1.call-start = ((), (), s32[]{:S(2)}) async-start(), calls=%async_computation.4 | async-start | bytes 25559040 | tf_op jit(solution)/shard_map/all_gather | solution.py:57
  36.2 665.2 %reduce-scatter.2.cloned.1.call-start = ((), (), s32[]{:S(2)}) async-start(), calls=%async_computation.2 | async-start | bytes 2359296 | tf_op jit(solution)/shard_map/reduce_scatter | solution.py:75
  469.5 2.5 copy-start.1
  476.1 2.5 copy-start.1
  482.7 2.5 copy-start.1
  489.3 2.5 copy-start.1
  495.9 2.5 copy-start.1
  502.6 2.5 copy-start.1
  509.2 2.5 copy-start.1
  515.8 2.5 copy-start.1
  522.4 2.5 copy-start.1
  529.0 2.5 copy-start.1
  535.7 2.5 copy-start.1
  542.3 2.5 copy-start.1
  548.9 2.5 copy-start.1
  555.5 2.5 copy-start.1
  562.1 2.5 copy-start.1
  568.8 2.5 copy-start.1
  575.4 2.5 copy-start.1
  582.0 2.5 copy-start.1
  588.6 2.5 copy-start.1
  595.2 2.5 copy-start.1
  (109 other events, 140.1 us)
Sparse Core Ops, SparseCore 0:
  9.0 16.1 all-gather.6
  35.6 184.4 all-gather.8
  222.8 184.6 all-gather.10
  687.5 13.8 reduce-scatter.1
where the time goes:
time: 710 us; the launch traced here: 708 us
  local copies, waits for them, and re-layouts  247 us (35%)
  waiting for transfers between devices  192 us (27%)
  blocking collectives  149 us (21%)
  matrix products  72.8 us (10%)
  other arithmetic  31.3 us (4%)
  between operations  13.2 us (2%)
    all_gather x1, blocking collectives, body(): clip_piece = lax.all_gather(clip_id, 'seq', axis=0, tiled=True)  149 us
    all_gather x1, waiting for transfers between devices, body(): value_piece = lax.all_gather(values_flat, 'seq', axis=0, tiled=True)  125 us
    unnamed x7, local copies, waits for them, and re-layouts  125 us
    dynamic_slice x64, local copies, waits for them, and re-layouts, body(): result, unused = lax.scan(tile_step, initial, tiles)  75.3 us
    while x288, local copies, waits for them, and re-layouts  45.6 us
    dot_general x32, matrix products, attend_tile(): jnp.einsum('qhk,khd->qhd', weights.astype(jnp.bfloat16), value_heads, pre...  34.7 us
    all_gather x1, waiting for transfers between devices, body(): key_piece = lax.all_gather(keys_flat, 'seq', axis=0, tiled=True)  33.7 us
    reduce_sum x32, other arithmetic, attend_tile(): totals = totals * factor + jnp.sum(weights, axis=-1)  24.8 us
  transfers between devices with their start and end apart: 4, of which 4 were waited for; matrix products, arithmetic and copies ran while one was open for 9% of the time, Pallas kernels for 0%

commit v1 on v0

v1 whole, which is shorter than its diff:
```python
import functools
import math

import jax
import jax.numpy as jnp
from jax import lax
from jax.experimental import pallas as pl
from jax.experimental.pallas import tpu as pltpu
from jax.sharding import Mesh
from jax.sharding import PartitionSpec as P

HEAD_DIM = 128
CHUNK = 1024
SEG = 128
NEG = -1e30
FLOOR = -1e29


def attend_kernel(info, q_ref, kv_ref, o_ref, keys, vals, scores):
    b1, b2, zl, y, x, c = [info[n] for n in range(6)]

    for zz in range(4):
        for cc in range(2):
            slot = ((zz & 1) ^ zl) * 2 + ((zz >> 1) ^ cc)
            for yy in range(4):
                at = ((zz * 4 + yy) * 2 + cc) * SEG
                keys[at : at + SEG, :] = kv_ref[yy * 2 + cc, slot, 0]
                vals[at : at + SEG, :HEAD_DIM] = kv_ref[yy * 2 + cc, slot, 1]
    vals[:, HEAD_DIM:] = jnp.ones((4096, HEAD_DIM), jnp.bfloat16)

    def below(bound):
        return (bound // 1024) * 256 + jnp.clip(bound % 1024 - x * 256, 0, 256)

    n1, n2 = below(b1), below(b2)
    row = lax.broadcasted_iota(jnp.int32, (256, 1), 0)
    eye = (
        lax.broadcasted_iota(jnp.int32, (SEG, SEG), 0)
        == lax.broadcasted_iota(jnp.int32, (SEG, SEG), 1)
    ).astype(jnp.float32)

    def lower(pos):
        return jnp.where(pos >= b2, n2, jnp.where(pos >= b1, n1, 0))

    def upper(pos):
        return jnp.where(pos >= b2, 4096, jnp.where(pos >= b1, n2, n1))

    def tile(t, carry):
        zz, xp = t // 2, t % 2
        slot = ((zz & 1) ^ zl) * 2 + ((zz >> 1) ^ c)
        q = jnp.concatenate([q_ref[2 * xp, slot], q_ref[2 * xp + 1, slot]], axis=0)
        first = zz * 4096 + y * 1024 + xp * 512 + c * 128
        last = first + 256 + 127
        pos = first + row + jnp.where(row >= SEG, SEG, 0)
        low_row, high_row = lower(pos), upper(pos)
        low_all, high_all = lower(first), upper(last)
        low_in, high_in = lower(last), upper(first)
        start = (low_all // 256) * 256
        count = (high_all - start + CHUNK - 1) // CHUNK
        start = pl.multiple_of(jnp.minimum(start, 4096 - count * CHUNK), 256)

        def first_pass(i, top):
            at = pl.multiple_of(start + i * CHUNK, 256)
            s = lax.dot_general(
                q, keys[pl.ds(at, CHUNK), :], (((1,), (1,)), ((), ())), preferred_element_type=jnp.float32
            )

            def masked():
                index = at + lax.broadcasted_iota(jnp.int32, (256, CHUNK), 1)
                return jnp.where((index >= low_row) & (index < high_row), s, NEG)

            s = lax.cond((at >= low_in) & (at + CHUNK <= high_in), lambda: s, masked)
            scores[i] = s
            for n in range(CHUNK // 128):
                top = jnp.maximum(top, s[:, n * 128 : (n + 1) * 128])
            return top

        top = lax.fori_loop(0, count, first_pass, jnp.full((256, 128), NEG, jnp.float32))
        top = jnp.maximum(jnp.max(top, axis=1, keepdims=True), FLOOR)

        def second_pass(i, acc):
            at = pl.multiple_of(start + i * CHUNK, 256)
            weights = jnp.exp(scores[i] - top).astype(jnp.bfloat16)
            return acc + jnp.dot(weights, vals[pl.ds(at, CHUNK), :], preferred_element_type=jnp.float32)

        acc = lax.fori_loop(0, count, second_pass, jnp.zeros((256, 256), jnp.float32))
        total = jnp.maximum(acc[:, HEAD_DIM:], 1e-30)
        out = (acc[:, :HEAD_DIM] / total).astype(jnp.bfloat16)
        level = top + jnp.log(total)
        for half in range(2):
            rel = (2 * xp + half - x + 4) % 4
            o_ref[rel, slot] = out[half * SEG : (half + 1) * SEG]
            line = jnp.sum(level[half * SEG : (half + 1) * SEG] * eye, axis=0, keepdims=True)
            high = line.astype(jnp.bfloat16).astype(jnp.float32)
            middle = (line - high).astype(jnp.bfloat16).astype(jnp.float32)
            rest = line - high - middle
            sub = lax.broadcasted_iota(jnp.int32, (16, 128), 0)
            parts = jnp.where(sub == 0, high, jnp.where(sub == 1, middle, jnp.where(sub == 2, rest, 0.0)))
            o_ref[rel, 4, pl.ds(pl.multiple_of(slot * 16, 16), 16), :] = parts.astype(jnp.bfloat16)
        return carry

    lax.fori_loop(0, 8, tile, 0)


def attend(info, q, kv):
    return pl.pallas_call(
        attend_kernel,
        out_shape=jax.ShapeDtypeStruct((4, 5, SEG, HEAD_DIM), jnp.bfloat16),
        in_specs=[
            pl.BlockSpec(memory_space=pltpu.SMEM),
            pl.BlockSpec(memory_space=pltpu.VMEM),
            pl.BlockSpec(memory_space=pltpu.VMEM),
        ],
        out_specs=pl.BlockSpec(memory_space=pltpu.VMEM),
        scratch_shapes=[
            pltpu.VMEM((4096, HEAD_DIM), jnp.bfloat16),
            pltpu.VMEM((4096, 2 * HEAD_DIM), jnp.bfloat16),
            pltpu.VMEM((4096 // CHUNK, 256, CHUNK), jnp.float32),
        ],
        compiler_params=pltpu.CompilerParams(vmem_limit_bytes=40 << 20),
        cost_estimate=pl.CostEstimate(
            flops=2 * 2 * 2048 * 4096 * 128 * 2, bytes_accessed=4 << 20, transcendentals=2048 * 4096
        ),
    )(info, q, kv)


def combine_kernel(*refs):
    out_ref = refs[-1]
    eye = (
        lax.broadcasted_iota(jnp.int32, (SEG, SEG), 0)
        == lax.broadcasted_iota(jnp.int32, (SEG, SEG), 1)
    ).astype(jnp.float32)
    for head in range(3):
        parts = refs[4 * head : 4 * head + 4]
        for slot in range(4):
            levels = []
            for part in parts:
                lines = part[4, slot * 16 : (slot + 1) * 16, :].astype(jnp.float32)
                levels.append(jnp.sum(lines, axis=0, keepdims=True))
            top = functools.reduce(jnp.maximum, levels)
            shares = [jnp.exp(level - top) for level in levels]
            total = functools.reduce(jnp.add, shares)
            spread = jnp.concatenate([eye * (share / total) for share in shares], axis=1)
            stacked = jnp.concatenate([part[slot] for part in parts], axis=0)
            mixed = jnp.dot(spread.astype(jnp.bfloat16), stacked, preferred_element_type=jnp.float32)
            out_ref[slot, :, head * HEAD_DIM : (head + 1) * HEAD_DIM] = mixed.astype(jnp.bfloat16)


def combine(blocks):
    return pl.pallas_call(
        combine_kernel,
        out_shape=jax.ShapeDtypeStruct((4, SEG, 3 * HEAD_DIM), jnp.bfloat16),
        in_specs=[pl.BlockSpec(memory_space=pltpu.VMEM)] * len(blocks),
        out_specs=pl.BlockSpec(memory_space=pltpu.VMEM),
        compiler_params=pltpu.CompilerParams(vmem_limit_bytes=32 << 20),
    )(*blocks)


SLOTS = [(a, b) for a in range(2) for b in range(2)]


def spread_pairs(a, b):
    pairs = []
    for z in range(4):
        for c in range(2):
            target = (2 * c + ((z % 2) ^ a)) * 2 + ((z // 2) ^ b)
            pairs.append((z * 2 + c, target))
    return pairs


def body(tokens, clip_id, w_qkv, w_out):
    z, y, x, c = [lax.axis_index(name) for name in ("z", "y", "x", "core")]
    zl, zh = z % 2, z // 2
    swap = [(0, 1), (1, 0)]

    counts = jnp.stack([jnp.sum(clip_id < 1), jnp.sum(clip_id < 2)]).astype(jnp.int32)
    bounds = lax.psum(counts, ("z", "y", "x"))
    info = jnp.concatenate([bounds, jnp.stack([zl, y, x, c]).astype(jnp.int32)])

    other = lax.ppermute(tokens, "core", swap)
    both = jnp.where(c == 0, jnp.concatenate([tokens, other], 1), jnp.concatenate([other, tokens], 1))
    stacked = jnp.einsum("td,sdc->stc", both, w_qkv, preferred_element_type=jnp.float32)
    scale = jnp.array([1.0 / math.sqrt(HEAD_DIM), 1.0, 1.0], jnp.float32)[:, None, None]
    stacked = (stacked * scale).astype(jnp.bfloat16)

    arrived = []
    for a, b in SLOTS:
        block = lax.dynamic_slice(stacked, (0, (zh ^ b) * SEG, (zl ^ a) * 384), (3, SEG, 384))
        arrived.append(lax.ppermute(block, ("z", "core"), spread_pairs(a, b)))

    results = []
    for head in range(3):
        cols = slice(head * HEAD_DIM, (head + 1) * HEAD_DIM)
        own_kv = jnp.stack([block[1:, :, cols] for block in arrived])
        own_q = jnp.stack([block[0, :, cols] for block in arrived])
        kv = lax.all_gather(own_kv, ("y", "core"), axis=0)
        q = lax.all_gather(own_q, "x", axis=0)
        out = attend(info, q, kv)
        results.append(out[0])
        for step in (1, 2, 3):
            results.append(lax.ppermute(out[step], "x", [(n, (n + step) % 4) for n in range(4)]))
    mixed = combine(results)

    back = []
    for index, (a, b) in enumerate(SLOTS):
        pairs = [(target, source) for source, target in spread_pairs(a, b)]
        back.append(lax.ppermute(mixed[index], ("z", "core"), pairs))
    rows = []
    for half in range(2):
        by_a = [jnp.where(zh == half, back[2 * a], back[2 * a + 1]) for a in range(2)]
        rows.append(
            jnp.concatenate([jnp.where(zl == 0, by_a[0], by_a[1]), jnp.where(zl == 0, by_a[1], by_a[0])], 1)
        )
    attended = jnp.concatenate(rows, axis=0)
    half_cols = w_out.shape[1] // 2
    w_there = lax.dynamic_slice(w_out, (0, (1 - c) * half_cols), (w_out.shape[0], half_cols))
    w_here = lax.dynamic_slice(w_out, (0, c * half_cols), (w_out.shape[0], half_cols))
    there = jnp.dot(attended, w_there, preferred_element_type=jnp.float32).astype(jnp.bfloat16)
    received = lax.ppermute(there, "core", swap)
    here = jnp.dot(attended, w_here, preferred_element_type=jnp.float32)
    return (here + received.astype(jnp.float32)).astype(jnp.bfloat16)


def solution(mesh):
    fine = Mesh(mesh.devices.reshape(4, 4, 4, 2), ("z", "y", "x", "core"))
    seq = ("z", "y", "x")
    in_specs = (P(seq, "core"), P(seq), P(None, None, "core"), P("core", None))
    return jax.shard_map(body, mesh=fine, in_specs=in_specs, out_specs=P(seq, "core"), check_vma=False)
```

time: 710 us -> 230 us (0.32)
  local copies, waits for them, and re-layouts: 247 us -> 5.42 us
  waiting for transfers between devices: 192 us -> 27.5 us
  blocking collectives: 149 us -> 50.1 us
  Pallas kernels: 0 us -> 75 us
  matrix products: 72.8 us -> 15.1 us
  starting transfers between devices: 0.12 us -> 42 us
  other arithmetic: 31.3 us -> 4.4 us
    all_gather x3, waiting for transfers between devices: 177 us -> 0.01 us  [body(): kv = lax.all_gather(own_kv, ('y', 'core'), axis=0)]
    unnamed x7 -> x8, local copies, waits for them, and re-layouts: 125 us -> 4.78 us
    all_gather x1 -> x3, blocking collectives: 149 us -> 31.5 us  [body(): q = lax.all_gather(own_q, 'x', axis=0)]
    dynamic_slice x64 -> x1, local copies, waits for them, and re-layouts: 75.3 us -> 0.15 us  [body(): lax.dynamic_slice(stacked, (0, (zh ^ b) * SEG, (zl ^ a) * 384), (3, SEG,...]
    pallas_call x0 -> x4, Pallas kernels: none -> 75 us  [the longest x3 74.4 us: attend(): pl.pallas_call(attend_kernel, out_shape=jax.ShapeDtypeStruct((4, 5, SEG,...]
    dot_general x66 -> x3, matrix products: 72.8 us -> 15.1 us  [the longest x1 9.34 us: body(): jnp.einsum('td,sdc->stc', both, w_qkv, preferred_element_type=jnp.float32)]
    while x288 -> x0, local copies, waits for them, and re-layouts: 45.6 us -> none
    ppermute x0 -> x19, starting transfers between devices: none -> 41.9 us  [the longest x4 24.6 us: body(): back.append(lax.ppermute(mixed[index], ('z', 'core'), pairs))]
  transfers between devices with their start and end apart: 4 -> 22, of which waited for: 4 -> 11; matrix products, arithmetic and copies ran while one was open for 9% -> 2% of each run, Pallas kernels for 0% -> 32%
where the time goes in v1:
time: 230 us; the launch traced here: 233 us
  Pallas kernels  75 us (33%)
  blocking collectives  50.1 us (22%)
  starting transfers between devices  42 us (18%)
  waiting for transfers between devices  27.5 us (12%)
  matrix products  15.1 us (7%)
  between operations  13.4 us (6%)
  local copies, waits for them, and re-layouts  5.42 us (2%)
  other arithmetic  4.4 us (2%)
    pallas_call x3, Pallas kernels, attend(): pl.pallas_call(attend_kernel, out_shape=jax.ShapeDtypeStruct((4, 5, SEG,...  74.4 us
    all_gather x3, blocking collectives, body(): q = lax.all_gather(own_q, 'x', axis=0)  31.5 us
    ppermute x4, starting transfers between devices, body(): back.append(lax.ppermute(mixed[index], ('z', 'core'), pairs))  24.6 us
    psum x1, blocking collectives, body(): bounds = lax.psum(counts, ('z', 'y', 'x'))  18.6 us
    ppermute x4, waiting for transfers between devices, body(): arrived.append(lax.ppermute(block, ('z', 'core'), spread_pairs(a, b)))  13.8 us
    ppermute x9, starting transfers between devices, body(): lax.ppermute(out[step], 'x', [(n, (n + step) % 4) for n in range(4)])  9.35 us
    dot_general x1, matrix products, body(): jnp.einsum('td,sdc->stc', both, w_qkv, preferred_element_type=jnp.float32)  9.34 us
    ppermute x4, starting transfers between devices, body(): arrived.append(lax.ppermute(block, ('z', 'core'), spread_pairs(a, b)))  6.5 us
  transfers between devices with their start and end apart: 22, of which 11 were waited for; matrix products, arithmetic and copies ran while one was open for 2% of the time, Pallas kernels for 32%

profile of v1, /device:TPU:1, one launch (start us, length us, event | category | flops | bytes accessed | tf_op | source)
XLA Modules:
  0.0 232.9 jit_solution(1500251579444689217)
XLA Ops:
  8.0 2.1 collective-permute-done
  10.1 9.3 %multiply_convert_fusion = bf16[256,3,768]{2,0,1:T(8,128)(2,1)S(1)} fusion(bf16[3,3072,768]{2,1,0:T(8,128)(2,1)} %param.7, bf16[256,1536]{1,0:T(8,128)(2,1)S(1)} %collective-permute-done, bf16[256,1536]{1,0:T(8,128)(2,1)} %param.5, pred[]{:T(512)S(6)} %eq.21, f32[3]{0:T(128)} %constant.57.clone), kind=kOutput, calls=%fused_computation.4 | convolution fusion | flops 3632136192 | bytes 16908300 | tf_op jit(solution)/shard_map/td,sdc->stc/dot_general | solution.py:181
  19.6 5.8 %collective-permute-start.1 = (bf16[3,128,384]{2,1,0:T(8,128)(2,1)S(1)}, bf16[3,128,384]{2,1,0:T(8,128)(2,1)S(1)}, u32[]{:S(2)}, u32[]{:S(2)}) collective-permute-start(bf16[3,128,384]{2,1,0:T(8,128)(2,1)S(1)} %get-tuple-element.7), channel_id=1, source_target_pairs={{0,0},{1,64},{32,32},{33,96},{64,1},{65,65},{96,33},{97,97},{2,2},... | collective-permute-start | bytes 884744 | tf_op jit(solution)/shard_map/ppermute | solution.py:188
  26.1 5.3 %collective-permute-done.1 = bf16[3,128,384]{2,1,0:T(8,128)(2,1)S(1)} collective-permute-done((bf16[3,128,384]{2,1,0:T(8,128)(2,1)S(1)}, bf16[3,128,384]{2,1,0:T(8,128)(2,1)S(1)}, u32[]{:S(2)}, u32[]{:S(2)}) %collective-permute-start.1) | collective-permute-done | bytes 294944 | tf_op jit(solution)/shard_map/ppermute | solution.py:188
  31.4 5.4 %collective-permute-done.2 = bf16[3,128,384]{2,1,0:T(8,128)(2,1)S(1)} collective-permute-done((bf16[3,128,384]{2,1,0:T(8,128)(2,1)S(1)}, bf16[3,128,384]{2,1,0:T(8,128)(2,1)S(1)}, u32[]{:S(2)}, u32[]{:S(2)}) %collective-permute-start.2) | collective-permute-done | bytes 294944 | tf_op jit(solution)/shard_map/ppermute | solution.py:188
  36.9 3.2 %collective-permute-done.4 = bf16[3,128,384]{2,1,0:T(8,128)(2,1)S(1)} collective-permute-done((bf16[3,128,384]{2,1,0:T(8,128)(2,1)S(1)}, bf16[3,128,384]{2,1,0:T(8,128)(2,1)S(1)}, u32[]{:S(2)}, u32[]{:S(2)}) %collective-permute-start.4) | collective-permute-done | bytes 294944 | tf_op jit(solution)/shard_map/ppermute | solution.py:188
  43.8 18.6 %psum.7 = s32[2]{0:T(128)S(1)} all-reduce(s32[2]{0:T(128)S(1)} %pad_add_fusion), channel_id=1, replica_groups=mesh['z'=4,'y'=4,'x'=4,'core'=2] {'z','y','x'}, use_global_device_ids=true, to_apply=%region_2.3 | all-reduce | flops 2 | bytes 16 | tf_op jit(solution)/shard_map/psum | solution.py:176
  63.4 9.9 %all-gather.4 = bf16[16,128,128]{2,1,0:T(8,128)(2,1)S(1)} all-gather(bf16[4,128,128]{2,1,0:T(8,128)(2,1)S(1)} %pad_maximum_fusion.5), channel_id=6, replica_groups=mesh['z'=4,'y'=4,'x'=4,'core'=2] {'x'}, dimensions={0}, use_global_device_ids=true | all-gather | bytes 655360 | tf_op jit(solution)/shard_map/all_gather | solution.py:196
  73.3 10.9 %all-gather.2 = bf16[16,128,128]{2,1,0:T(8,128)(2,1)S(1)} all-gather(bf16[4,128,128]{2,1,0:T(8,128)(2,1)S(1)} %pad_maximum_fusion.4), channel_id=4, replica_groups=mesh['z'=4,'y'=4,'x'=4,'core'=2] {'x'}, dimensions={0}, use_global_device_ids=true | all-gather | bytes 655360 | tf_op jit(solution)/shard_map/all_gather | solution.py:196
  84.2 10.7 %all-gather = bf16[16,128,128]{2,1,0:T(8,128)(2,1)S(1)} all-gather(bf16[4,128,128]{2,1,0:T(8,128)(2,1)S(1)} %pad_maximum_fusion.3), channel_id=2, replica_groups=mesh['z'=4,'y'=4,'x'=4,'core'=2] {'x'}, dimensions={0}, use_global_device_ids=true | all-gather | bytes 655360 | tf_op jit(solution)/shard_map/all_gather | solution.py:196
  96.5 24.8 %shard_map.57 = bf16[4,5,128,128]{3,2,1,0:T(8,128)(2,1)S(1)} custom-call(s32[6]{0:T(128)S(1)} %concatenate.18.info, bf16[4,4,128,128]{3,2,1,0:T(8,128)(2,1)S(1)} %bitcast.82, bf16[8,4,2,128,128]{4,3,2,1,0:T(8,128)(2,1)S(1)} %bitcast.84), custom_call_target="tpu_custom_call" | custom-call | flops 8589934592 | bytes 4194304 | tf_op jit(solution)/shard_map/pallas_call | solution.py:105
  121.5 2.6 %collective-permute-start.13 = (bf16[5,128,128]{2,1,0:T(8,128)(2,1)S(1)}, bf16[5,128,128]{2,1,0:T(8,128)(2,1)S(1)}, u32[]{:S(2)}, u32[]{:S(2)}) collective-permute-start(bf16[5,128,128]{2,1,0:T(8,128)(2,1)S(1)} %get-tuple-element.11), channel_id=1, source_target_pairs={{0,6},{2,0},{4,2},{6,4},{1,7},{3,1},{5,3},{7,5},{8,14},{10,8},{12,... | collective-permute-start | bytes 491528 | tf_op jit(solution)/shard_map/ppermute | solution.py:200
  125.7 24.8 %shard_map.56 = bf16[4,5,128,128]{3,2,1,0:T(8,128)(2,1)S(1)} custom-call(s32[6]{0:T(128)S(1)} %concatenate.18.info, bf16[4,4,128,128]{3,2,1,0:T(8,128)(2,1)S(1)} %bitcast.81, bf16[8,4,2,128,128]{4,3,2,1,0:T(8,128)(2,1)S(1)} %bitcast.83), custom_call_target="tpu_custom_call" | custom-call | flops 8589934592 | bytes 4194304 | tf_op jit(solution)/shard_map/pallas_call | solution.py:105
  153.7 24.8 %shard_map.55 = bf16[4,5,128,128]{3,2,1,0:T(8,128)(2,1)S(1)} custom-call(s32[6]{0:T(128)S(1)} %concatenate.18.info, bf16[4,4,128,128]{3,2,1,0:T(8,128)(2,1)S(1)} %bitcast.80, bf16[8,4,2,128,128]{4,3,2,1,0:T(8,128)(2,1)S(1)} %bitcast.85), custom_call_target="tpu_custom_call" | custom-call | flops 8589934592 | bytes 4194304 | tf_op jit(solution)/shard_map/pallas_call | solution.py:105
  178.8 2.9 %collective-permute-start.6 = (bf16[5,128,128]{2,1,0:T(8,128)(2,1)S(1)}, bf16[5,128,128]{2,1,0:T(8,128)(2,1)S(1)}, u32[]{:S(2)}, u32[]{:S(2)}) collective-permute-start(bf16[5,128,128]{2,1,0:T(8,128)(2,1)S(1)} %get-tuple-element.20), channel_id=1, source_target_pairs={{0,4},{2,6},{4,0},{6,2},{1,5},{3,7},{5,1},{7,3},{8,12},{10,14},{12... | collective-permute-start | bytes 491528 | tf_op jit(solution)/shard_map/ppermute | solution.py:200
  181.7 2.0 collective-permute-start.7
  185.9 2.0 collective-permute-done.6.refs_2_
  188.5 22.4 %collective-permute-start.14 = (bf16[128,384]{1,0:T(8,128)(2,1)S(1)}, bf16[128,384]{1,0:T(8,128)(2,1)S(1)}, u32[]{:S(2)}, u32[]{:S(2)}) collective-permute-start(bf16[128,384]{1,0:T(8,128)(2,1)S(1)} %get-tuple-element.30), channel_id=1, source_target_pairs={{0,0},{64,1},{32,32},{96,33},{1,64},{65,65},{33,96},{97,97},{2,2},... | collective-permute-start | bytes 294920 | tf_op jit(solution)/shard_map/ppermute | solution.py:206
  211.2 1.9 collective-permute-start.17
  213.3 2.8 %collective-permute-done.15 = bf16[128,384]{1,0:T(8,128)(2,1)S(1)} collective-permute-done((bf16[128,384]{1,0:T(8,128)(2,1)S(1)}, bf16[128,384]{1,0:T(8,128)(2,1)S(1)}, u32[]{:S(2)}, u32[]{:S(2)}) %collective-permute-start.15) | collective-permute-done | bytes 98336 | tf_op jit(solution)/shard_map/ppermute | solution.py:206
  216.1 2.0 collective-permute-done.16
  218.2 2.4 %convolution_convert_fusion = bf16[256,1536]{1,0:T(8,128)(2,1)S(1)} fusion(bf16[768,3072]{1,0:T(8,128)(2,1)} %param.8, s32[]{:T(128)S(6)} %select_n.101, bf16[128,384]{1,0:T(8,128)(2,1)S(1)} %get-tuple-element.26, bf16[128,384]{1,0:T(8,128)(2,1)S(1)} %get-tuple-element.25, bf16[128,384]{1,0:T(8,128)(2,1)S(1)} %get-tuple-element.24, ...), kind=kOutput, calls=%fused_computation | convolution fusion | flops 605945856 | bytes 3538948 | tf_op jit(solution)/shard_map/dot_general | solution.py:217
  220.7 2.3 collective-permute-done.18
  223.0 3.3 %add_convert_fusion = bf16[256,1536]{1,0:T(8,128)(2,1)} fusion(bf16[256,1536]{1,0:T(8,128)(2,1)S(1)} %collective-permute-done.18, bf16[768,3072]{1,0:T(8,128)(2,1)} %param.8, s32[]{:T(128)S(6)} %select_n.100, bf16[128,384]{1,0:T(8,128)(2,1)S(1)} %get-tuple-element.26, bf16[128,384]{1,0:T(8,128)(2,1)S(1)} %get-tuple-element.25, ...), kind=kOutput, calls=%fused_computation.12 | convolution fusion | flops 606732288 | bytes 4325380 | tf_op jit(solution)/shard_map/dot_general | solution.py:219
  (65 shorter events, 17.1 us)
Async XLA Ops:
  6.5 88.4 %all-gather.14.cloned.1.call-start = ((), (), s32[]{:S(2)}) async-start(), calls=%async_computation.2 | async-start | bytes 2359296 | tf_op jit(solution)/shard_map/all_gather | solution.py:195
  6.5 3.5 %collective-permute-start = (bf16[256,1536]{1,0:T(8,128)(2,1)}, bf16[256,1536]{1,0:T(8,128)(2,1)S(1)}, u32[]{:S(2)}, u32[]{:S(2)}) collective-permute-start(bf16[256,1536]{1,0:T(8,128)(2,1)} %param.5), channel_id=1, source_target_pairs={{0,1},{1,0},{2,3},{3,2},{4,5},{5,4},{6,7},{7,6},{8,9},{9,8},{10,11... | collective-permute-start | bytes 2359304 | tf_op jit(solution)/shard_map/ppermute | solution.py:179
  19.4 22.3 %copy-start.3 = (s32[256]{0:T(256)S(1)}, s32[256]{0:T(256)}, u32[]{:S(2)}) copy-start(s32[256]{0:T(256)} %param.6) | copy-start | bytes 3076
  19.6 11.8 %collective-permute-start.1 = (bf16[3,128,384]{2,1,0:T(8,128)(2,1)S(1)}, bf16[3,128,384]{2,1,0:T(8,128)(2,1)S(1)}, u32[]{:S(2)}, u32[]{:S(2)}) collective-permute-start(bf16[3,128,384]{2,1,0:T(8,128)(2,1)S(1)} %get-tuple-element.7), channel_id=1, source_target_pairs={{0,0},{1,64},{32,32},{33,96},{64,1},{65,65},{96,33},{97,97},{2,2},... | collective-permute-start | bytes 884744 | tf_op jit(solution)/shard_map/ppermute | solution.py:188
  25.5 11.3 %collective-permute-start.2 = (bf16[3,128,384]{2,1,0:T(8,128)(2,1)S(1)}, bf16[3,128,384]{2,1,0:T(8,128)(2,1)S(1)}, u32[]{:S(2)}, u32[]{:S(2)}) collective-permute-start(bf16[3,128,384]{2,1,0:T(8,128)(2,1)S(1)} %get-tuple-element.10), channel_id=1, source_target_pairs={{0,1},{1,65},{32,33},{33,97},{64,0},{65,64},{96,32},{97,96},{2,3},... | collective-permute-start | bytes 884744 | tf_op jit(solution)/shard_map/ppermute | solution.py:188
  25.5 11.3 %collective-permute-start.3 = (bf16[3,128,384]{2,1,0:T(8,128)(2,1)S(1)}, bf16[3,128,384]{2,1,0:T(8,128)(2,1)S(1)}, u32[]{:S(2)}, u32[]{:S(2)}) collective-permute-start(bf16[3,128,384]{2,1,0:T(8,128)(2,1)S(1)} %get-tuple-element.9), channel_id=1, source_target_pairs={{0,32},{1,96},{32,0},{33,64},{64,33},{65,97},{96,1},{97,65},{2,34}... | collective-permute-start | bytes 884744 | tf_op jit(solution)/shard_map/ppermute | solution.py:188
  26.1 14.0 %collective-permute-start.4 = (bf16[3,128,384]{2,1,0:T(8,128)(2,1)S(1)}, bf16[3,128,384]{2,1,0:T(8,128)(2,1)S(1)}, u32[]{:S(2)}, u32[]{:S(2)}) collective-permute-start(bf16[3,128,384]{2,1,0:T(8,128)(2,1)S(1)} %get-tuple-element.8), channel_id=1, source_target_pairs={{0,33},{1,97},{32,1},{33,65},{64,32},{65,96},{96,0},{97,64},{2,35}... | collective-permute-start | bytes 884744 | tf_op jit(solution)/shard_map/ppermute | solution.py:188
  40.9 83.2 %all-gather.12.cloned.1.call-start = ((), (), s32[]{:S(2)}) async-start(), calls=%async_computation.1 | async-start | bytes 2359296 | tf_op jit(solution)/shard_map/all_gather | solution.py:195
  41.7 110.4 %all-gather.10.cloned.1.call-start = ((), (), s32[]{:S(2)}) async-start(), calls=%async_computation | async-start | bytes 2359296 | tf_op jit(solution)/shard_map/all_gather | solution.py:195
  94.9 1.6 copy-start.1
  121.4 57.2 %collective-permute-start.11 = (bf16[5,128,128]{2,1,0:T(8,128)(2,1)S(1)}, bf16[5,128,128]{2,1,0:T(8,128)(2,1)S(1)}, u32[]{:S(2)}, u32[]{:S(2)}) collective-permute-start(bf16[5,128,128]{2,1,0:T(8,128)(2,1)S(1)} %get-tuple-element.13), channel_id=1, source_target_pairs={{0,2},{2,4},{4,6},{6,0},{1,3},{3,5},{5,7},{7,1},{8,10},{10,12},{12... | collective-permute-start | bytes 491528 | tf_op jit(solution)/shard_map/ppermute | solution.py:200
  121.5 57.2 %collective-permute-start.12 = (bf16[5,128,128]{2,1,0:T(8,128)(2,1)S(1)}, bf16[5,128,128]{2,1,0:T(8,128)(2,1)S(1)}, u32[]{:S(2)}, u32[]{:S(2)}) collective-permute-start(bf16[5,128,128]{2,1,0:T(8,128)(2,1)S(1)} %get-tuple-element.12), channel_id=1, source_target_pairs={{0,4},{2,6},{4,0},{6,2},{1,5},{3,7},{5,1},{7,3},{8,12},{10,14},{12... | collective-permute-start | bytes 491528 | tf_op jit(solution)/shard_map/ppermute | solution.py:200
  121.5 57.2 %collective-permute-start.13 = (bf16[5,128,128]{2,1,0:T(8,128)(2,1)S(1)}, bf16[5,128,128]{2,1,0:T(8,128)(2,1)S(1)}, u32[]{:S(2)}, u32[]{:S(2)}) collective-permute-start(bf16[5,128,128]{2,1,0:T(8,128)(2,1)S(1)} %get-tuple-element.11), channel_id=1, source_target_pairs={{0,6},{2,0},{4,2},{6,4},{1,7},{3,1},{5,3},{7,5},{8,14},{10,8},{12,... | collective-permute-start | bytes 491528 | tf_op jit(solution)/shard_map/ppermute | solution.py:200
  150.6 31.1 %collective-permute-start.10 = (bf16[5,128,128]{2,1,0:T(8,128)(2,1)S(1)}, bf16[5,128,128]{2,1,0:T(8,128)(2,1)S(1)}, u32[]{:S(2)}, u32[]{:S(2)}) collective-permute-start(bf16[5,128,128]{2,1,0:T(8,128)(2,1)S(1)} %get-tuple-element.15), channel_id=1, source_target_pairs={{0,6},{2,0},{4,2},{6,4},{1,7},{3,1},{5,3},{7,5},{8,14},{10,8},{12,... | collective-permute-start | bytes 491528 | tf_op jit(solution)/shard_map/ppermute | solution.py:200
  150.6 33.0 %collective-permute-start.8 = (bf16[5,128,128]{2,1,0:T(8,128)(2,1)S(1)}, bf16[5,128,128]{2,1,0:T(8,128)(2,1)S(1)}, u32[]{:S(2)}, u32[]{:S(2)}) collective-permute-start(bf16[5,128,128]{2,1,0:T(8,128)(2,1)S(1)} %get-tuple-element.17), channel_id=1, source_target_pairs={{0,2},{2,4},{4,6},{6,0},{1,3},{3,5},{5,7},{7,1},{8,10},{10,12},{12... | collective-permute-start | bytes 491528 | tf_op jit(solution)/shard_map/ppermute | solution.py:200
  178.6 5.9 %collective-permute-start.9 = (bf16[5,128,128]{2,1,0:T(8,128)(2,1)S(1)}, bf16[5,128,128]{2,1,0:T(8,128)(2,1)S(1)}, u32[]{:S(2)}, u32[]{:S(2)}) collective-permute-start(bf16[5,128,128]{2,1,0:T(8,128)(2,1)S(1)} %get-tuple-element.16), channel_id=1, source_target_pairs={{0,4},{2,6},{4,0},{6,2},{1,5},{3,7},{5,1},{7,3},{8,12},{10,14},{12... | collective-permute-start | bytes 491528 | tf_op jit(solution)/shard_map/ppermute | solution.py:200
  178.7 7.2 %collective-permute-start.5 = (bf16[5,128,128]{2,1,0:T(8,128)(2,1)S(1)}, bf16[5,128,128]{2,1,0:T(8,128)(2,1)S(1)}, u32[]{:S(2)}, u32[]{:S(2)}) collective-permute-start(bf16[5,128,128]{2,1,0:T(8,128)(2,1)S(1)} %get-tuple-element.21), channel_id=1, source_target_pairs={{0,2},{2,4},{4,6},{6,0},{1,3},{3,5},{5,7},{7,1},{8,10},{10,12},{12... | collective-permute-start | bytes 491528 | tf_op jit(solution)/shard_map/ppermute | solution.py:200
  178.8 9.1 %collective-permute-start.6 = (bf16[5,128,128]{2,1,0:T(8,128)(2,1)S(1)}, bf16[5,128,128]{2,1,0:T(8,128)(2,1)S(1)}, u32[]{:S(2)}, u32[]{:S(2)}) collective-permute-start(bf16[5,128,128]{2,1,0:T(8,128)(2,1)S(1)} %get-tuple-element.20), channel_id=1, source_target_pairs={{0,4},{2,6},{4,0},{6,2},{1,5},{3,7},{5,1},{7,3},{8,12},{10,14},{12... | collective-permute-start | bytes 491528 | tf_op jit(solution)/shard_map/ppermute | solution.py:200
  181.7 6.2 %collective-permute-start.7 = (bf16[5,128,128]{2,1,0:T(8,128)(2,1)S(1)}, bf16[5,128,128]{2,1,0:T(8,128)(2,1)S(1)}, u32[]{:S(2)}, u32[]{:S(2)}) collective-permute-start(bf16[5,128,128]{2,1,0:T(8,128)(2,1)S(1)} %get-tuple-element.19), channel_id=1, source_target_pairs={{0,6},{2,0},{4,2},{6,4},{1,7},{3,1},{5,3},{7,5},{8,14},{10,8},{12,... | collective-permute-start | bytes 491528 | tf_op jit(solution)/shard_map/ppermute | solution.py:200
  188.5 24.7 %collective-permute-start.14 = (bf16[128,384]{1,0:T(8,128)(2,1)S(1)}, bf16[128,384]{1,0:T(8,128)(2,1)S(1)}, u32[]{:S(2)}, u32[]{:S(2)}) collective-permute-start(bf16[128,384]{1,0:T(8,128)(2,1)S(1)} %get-tuple-element.30), channel_id=1, source_target_pairs={{0,0},{64,1},{32,32},{96,33},{1,64},{65,65},{33,96},{97,97},{2,2},... | collective-permute-start | bytes 294920 | tf_op jit(solution)/shard_map/ppermute | solution.py:206
  211.0 5.1 %collective-permute-start.15 = (bf16[128,384]{1,0:T(8,128)(2,1)S(1)}, bf16[128,384]{1,0:T(8,128)(2,1)S(1)}, u32[]{:S(2)}, u32[]{:S(2)}) collective-permute-start(bf16[128,384]{1,0:T(8,128)(2,1)S(1)} %get-tuple-element.29), channel_id=1, source_target_pairs={{1,0},{65,1},{33,32},{97,33},{0,64},{64,65},{32,96},{96,97},{3,2},... | collective-permute-start | bytes 294920 | tf_op jit(solution)/shard_map/ppermute | solution.py:206
  211.1 7.1 %collective-permute-start.16 = (bf16[128,384]{1,0:T(8,128)(2,1)S(1)}, bf16[128,384]{1,0:T(8,128)(2,1)S(1)}, u32[]{:S(2)}, u32[]{:S(2)}) collective-permute-start(bf16[128,384]{1,0:T(8,128)(2,1)S(1)} %get-tuple-element.28), channel_id=1, source_target_pairs={{32,0},{96,1},{0,32},{64,33},{33,64},{97,65},{1,96},{65,97},{34,2}... | collective-permute-start | bytes 294920 | tf_op jit(solution)/shard_map/ppermute | solution.py:206
  211.2 7.0 %collective-permute-start.17 = (bf16[128,384]{1,0:T(8,128)(2,1)S(1)}, bf16[128,384]{1,0:T(8,128)(2,1)S(1)}, u32[]{:S(2)}, u32[]{:S(2)}) collective-permute-start(bf16[128,384]{1,0:T(8,128)(2,1)S(1)} %get-tuple-element.27), channel_id=1, source_target_pairs={{33,0},{97,1},{1,32},{65,33},{32,64},{96,65},{0,96},{64,97},{35,2}... | collective-permute-start | bytes 294920 | tf_op jit(solution)/shard_map/ppermute | solution.py:206
  220.7 2.4 %collective-permute-start.18 = (bf16[256,1536]{1,0:T(8,128)(2,1)S(1)}, bf16[256,1536]{1,0:T(8,128)(2,1)S(1)}, u32[]{:S(2)}, u32[]{:S(2)}) collective-permute-start(bf16[256,1536]{1,0:T(8,128)(2,1)S(1)} %convolution_convert_fusion), channel_id=1, source_target_pairs={{0,1},{1,0},{2,3},{3,2},{4,5},{5,4},{6,7},{7,6},{8,9},{9,8},{10,11... | collective-permute-start | bytes 2359304 | tf_op jit(solution)/shard_map/ppermute | solution.py:218
  (2 other events, 3.2 us)
Sparse Core Ops, SparseCore 0:
  41.0 25.7 all-gather.13
  68.5 25.5 all-gather.11
  95.9 25.4 all-gather.9
